TPU v7x, 32 devices: a whole 2x2x4 slice. The times are simulated.
32 devices in a mesh: seq: 16 (over z, y, x), head: 2 (over core).
Axes of the slice: x: 2, y: 2, z: 4, core: 2. Of those that a mesh axis runs over, the one named last changes fastest.
Arguments:
- tokens: bfloat16 [2048, 2048], P('seq'), may hold values from -6 to 6
- norm1_gain: float32 [2048], replicated, may hold values from 0.1 to 1.9
- mix_weight: bfloat16 [4, 2048, 2048], P(None, 'seq', 'head'), may hold values from -0.125 to 0.125
- conv_weight: float32 [3, 4, 2048], P(None, None, 'head'), may hold values from -3 to 3
- decay_gap: float32 [2048], P('head'), may hold values from 0.00024414062 to 0.05
- group_gain: float32 [2048], P('head'), may hold values from 0.1 to 1.9
- out_weight: bfloat16 [2048, 2048], P('head', 'seq'), may hold values from -0.25 to 0.25
- norm2_gain: float32 [2048], replicated, may hold values from 0.1 to 1.9
- up_pair: bfloat16 [2, 2048, 5632], P(None, 'seq', 'head'), may hold values from -0.125 to 0.125
- down_weight: bfloat16 [5632, 2048], P('head', 'seq'), may hold values from -0.078125 to 0.078125
- cotangent: bfloat16 [2048, 2048], P('seq'), may hold values from -6 to 6
Outputs:
- block_out: float32 [2048, 2048], P('seq')
- grad_tokens: float32 [2048, 2048], P('seq')
- grad_norm1: float32 [2048], replicated
- grad_mix: float32 [4, 2048, 2048], P(None, 'seq', 'head')
- grad_conv: float32 [3, 4, 2048], P(None, None, 'head')
- grad_gap: float32 [2048], P('head')
- grad_group: float32 [2048], P('head')
- grad_out: float32 [2048, 2048], P('head', 'seq')
- grad_norm2: float32 [2048], replicated
- grad_up: float32 [2, 2048, 5632], P(None, 'seq', 'head')
- grad_down: float32 [5632, 2048], P('head', 'seq')
- inverse_rms: float32 [2, 2048], P(None, 'seq')
All inputs are finite; a program needn't handle non-finite values.
Results may differ from a plain program's by a relative error of at most 0.012.
Values may be sent and summed in bfloat16 or wider, within the bound.
No kernel may reach another device: no remote copies, remote signals or barrier semaphores. Data moves between devices by JAX's collectives and lax.ppermute only.
A program may use at most 320 MiB of HBM per device.

v0:
```python
import jax
import jax.numpy as jnp
from jax import lax
from jax.sharding import PartitionSpec as P

HEAD_DIM = 128
SPAN = 64
EPS_TOKEN = 1e-06
EPS_GROUP = 1e-05
HIGH = lax.Precision.HIGHEST


def from_behind(value, axis, steps):
    count = lax.axis_size(axis)
    first, last = (max(0, -steps), min(count, count - steps))
    return lax.ppermute(value, axis, [(source, source + steps) for source in range(first, last)])


def carried_in(array, axis, combine, identity, reverse):
    peers, here = (lax.axis_size(axis), lax.axis_index(axis))
    everything = jax.tree.map(lambda part: lax.all_gather(part, axis), array)
    start = jax.tree.map(
        lambda part, zero: jnp.broadcast_to(jnp.asarray(zero, part.dtype), part.shape),
        array,
        identity,
    )

    def turn(k, before):
        at = peers - 1 - k if reverse else k
        reached = at > here if reverse else at < here
        new = combine(before, jax.tree.map(lambda part: part[at], everything))
        return jax.tree.map(lambda a, b: jnp.where(reached, a, b), new, before)

    return lax.fori_loop(0, peers, turn, start)


def silu_grad(inputs_val):
    sigmoid_val = jax.nn.sigmoid(inputs_val)
    return sigmoid_val * (1.0 + inputs_val * (1.0 - sigmoid_val))


def token_norm(token_rows, gain_vec):
    inverse = lax.rsqrt(jnp.mean(token_rows * token_rows, axis=-1, keepdims=True) + EPS_TOKEN)
    return (token_rows * inverse * gain_vec, inverse)


def token_norm_back(token_rows, inverse, gain_vec, grad_in):
    scaled = grad_in * gain_vec
    dot_term = jnp.mean(scaled * token_rows, axis=-1, keepdims=True)
    grad_rows = inverse * scaled - token_rows * inverse * inverse * inverse * dot_term
    grad_gain = jnp.sum(grad_in * token_rows * inverse, axis=0)
    return (grad_rows, grad_gain)


def convolve(extended, conv_taps):
    length = extended.shape[1] - 3
    total = conv_taps[:, 0][:, None] * extended[:, 3:]
    for delay_step in range(1, 4):
        total = (
            total
            + conv_taps[:, delay_step][:, None]
            * extended[:, 3 - delay_step : 3 - delay_step + length]
        )
    return total


def gates(convolved, decay_gap):
    queries = jax.nn.silu(convolved[0])
    open_share = 1.0 - jax.nn.sigmoid(convolved[1])
    log_forget = jnp.log(1.0 - decay_gap * open_share)
    key_rows = decay_gap * open_share
    return (queries, log_forget, key_rows, convolved[2])


def span_step(carry_state, pieces):
    queries, log_forget, key_rows, values = pieces
    running = jnp.cumsum(log_forget, axis=0)
    decayed_query = queries * jnp.exp(running)
    lifted_key = key_rows * jnp.exp(-running)
    scores = jnp.einsum("thd,shd->hts", decayed_query, lifted_key, precision=HIGH)
    causal = jnp.arange(SPAN)[:, None] >= jnp.arange(SPAN)[None, :]
    scores = jnp.where(causal[None], scores, 0.0)
    mixed_out = jnp.einsum("hts,she->the", scores, values, precision=HIGH)
    mixed_out = mixed_out + jnp.einsum("thd,hde->the", decayed_query, carry_state, precision=HIGH)
    final_log = running[-1]
    carried = key_rows * jnp.exp(final_log[None] - running)
    carry_state = jnp.exp(final_log)[:, :, None] * carry_state + jnp.einsum(
        "thd,the->hde", carried, values, precision=HIGH
    )
    return (carry_state, mixed_out)


def local_mix(queries, log_forget, key_rows, values, state_in):
    length, heads_here, head_width = queries.shape
    blocks = length // SPAN

    def blocked(array):
        return array.reshape(blocks, SPAN, heads_here, head_width)

    state_out, mixed_out = lax.scan(
        jax.checkpoint(span_step),
        state_in,
        (blocked(queries), blocked(log_forget), blocked(key_rows), blocked(values)),
    )
    return (mixed_out.reshape(length, heads_here, head_width), state_out)


def running_log(log_forget):
    length = log_forget.shape[0]
    blocked = log_forget.reshape((length // SPAN, SPAN) + log_forget.shape[1:])
    inside = jnp.cumsum(blocked, axis=1)
    totals = inside[:, -1]
    before = jnp.cumsum(totals, axis=0) - totals
    return (inside + before[:, None]).reshape(log_forget.shape)


def group_gate(mixed_out, gate_rows, group_gain):
    inverse = lax.rsqrt(jnp.mean(mixed_out * mixed_out, axis=-1, keepdims=True) + EPS_GROUP)
    normed = (mixed_out * inverse).reshape(gate_rows.shape)
    return normed * group_gain * jax.nn.silu(gate_rows)


def split_heads(array):
    return array.reshape(array.shape[0], -1, HEAD_DIM)


def merge_heads(array):
    return array.reshape(array.shape[0], -1)


def combine_state(earlier, later):
    return (earlier[0] * later[0], later[0][..., None] * earlier[1] + later[1])


def head_total(partial_sum):
    share = lax.psum_scatter(partial_sum, "head", scatter_dimension=1, tiled=True)
    return lax.all_gather(share, "head", axis=1, tiled=True)


def shards(
    tokens,
    norm1_gain,
    mix_weight,
    conv_weight,
    decay_gap,
    group_gain,
    out_weight,
    norm2_gain,
    up_pair,
    down_weight,
    cotangent,
):
    mix_full, up_full, out_full, down_full = (
        lax.all_gather(mix_weight, "seq", axis=1, tiled=True),
        lax.all_gather(up_pair, "seq", axis=1, tiled=True),
        lax.all_gather(out_weight, "seq", axis=1, tiled=True),
        lax.all_gather(down_weight, "seq", axis=1, tiled=True),
    )
    token_rows = tokens.astype(jnp.float32)
    normed1, inverse1 = token_norm(token_rows, norm1_gain)
    normed1_low = normed1.astype(jnp.bfloat16)
    projected = jnp.einsum(
        "td,jdc->jtc", normed1_low, mix_full, preferred_element_type=jnp.float32
    ).astype(jnp.bfloat16)
    length = projected.shape[1]
    earlier_rows = from_behind(projected[:3, length - 3 :], "seq", 1)
    extended = jnp.concatenate([earlier_rows, projected[:3]], axis=1).astype(jnp.float32)
    convolved, conv_back = jax.vjp(convolve, extended, conv_weight)
    (queries, log_forget, key_rows, values), gate_back = jax.vjp(gates, convolved, decay_gap)
    query_heads = split_heads(queries)
    forget_heads = split_heads(log_forget)
    key_heads = split_heads(key_rows)
    value_heads = split_heads(values)
    log_total = running_log(forget_heads)
    last_log = log_total[-1]
    decay_dev = jnp.exp(last_log)
    own_state = jnp.einsum(
        "thd,the->hde", key_heads * jnp.exp(last_log[None] - log_total), value_heads, precision=HIGH
    )
    identity = (jnp.ones_like(decay_dev), jnp.zeros_like(own_state))
    prior_decay, state_in = carried_in(
        (decay_dev, own_state), "seq", combine_state, identity, False
    )
    (mixed_out, state_end), mix_back = jax.vjp(
        local_mix, query_heads, forget_heads, key_heads, value_heads, state_in
    )
    gate_rows = projected[3].astype(jnp.float32)
    gated, group_back = jax.vjp(group_gate, mixed_out, gate_rows, group_gain)
    gated_low = gated.astype(jnp.bfloat16)
    hidden = token_rows + head_total(
        jnp.dot(gated_low, out_full, preferred_element_type=jnp.float32)
    )
    normed2, inverse2 = token_norm(hidden, norm2_gain)
    normed2_low = normed2.astype(jnp.bfloat16)
    lifted = jnp.einsum("td,jdf->jtf", normed2_low, up_full, preferred_element_type=jnp.float32)
    gate_act = jax.nn.silu(lifted[0])
    inner_act = (gate_act * lifted[1]).astype(jnp.bfloat16)
    block_out = hidden + head_total(
        jnp.dot(inner_act, down_full, preferred_element_type=jnp.float32)
    )
    mix_again, up_again, out_again, down_again = (
        lax.all_gather(mix_weight, "seq", axis=1, tiled=True),
        lax.all_gather(up_pair, "seq", axis=1, tiled=True),
        lax.all_gather(out_weight, "seq", axis=1, tiled=True),
        lax.all_gather(down_weight, "seq", axis=1, tiled=True),
    )
    upstream = cotangent.astype(jnp.float32)
    grad_down = jnp.einsum("tf,td->fd", inner_act, cotangent, preferred_element_type=jnp.float32)
    grad_inner = jnp.einsum("td,fd->tf", cotangent, down_again, preferred_element_type=jnp.float32)
    grad_lifted = jnp.stack(
        [grad_inner * lifted[1] * silu_grad(lifted[0]), grad_inner * gate_act]
    ).astype(jnp.bfloat16)
    grad_up = jnp.einsum(
        "td,jtf->jdf", normed2_low, grad_lifted, preferred_element_type=jnp.float32
    )
    grad_normed2 = head_total(
        jnp.einsum("jtf,jdf->td", grad_lifted, up_again, preferred_element_type=jnp.float32)
    )
    grad_hidden_norm, grad_norm2 = token_norm_back(hidden, inverse2, norm2_gain, grad_normed2)
    grad_hidden = upstream + grad_hidden_norm
    grad_branch = grad_hidden.astype(jnp.bfloat16)
    grad_out = jnp.einsum("tc,td->cd", gated_low, grad_branch, preferred_element_type=jnp.float32)
    grad_gated = jnp.einsum("td,cd->tc", grad_branch, out_again, preferred_element_type=jnp.float32)
    grad_mixed, grad_gate_rows, grad_group = group_back(grad_gated)
    own_grad = jnp.einsum(
        "thd,the->hde", query_heads * jnp.exp(log_total), grad_mixed, precision=HIGH
    )
    later_decay, state_after = carried_in(
        (decay_dev, own_grad), "seq", combine_state, identity, True
    )
    grad_q, grad_f, grad_k, grad_v, grad_start = mix_back((grad_mixed, state_after))
    grad_convolved, grad_gap = gate_back(
        (merge_heads(grad_q), merge_heads(grad_f), merge_heads(grad_k), merge_heads(grad_v))
    )
    grad_extended, grad_conv = conv_back(grad_convolved)
    later_edge = from_behind(grad_extended[:, :3].astype(jnp.bfloat16), "seq", -1).astype(
        jnp.float32
    )
    edge_pad = jnp.concatenate(
        [jnp.zeros((3, length - 3, later_edge.shape[2]), jnp.float32), later_edge], axis=1
    )
    grad_conv_rows = grad_extended[:, 3:] + edge_pad
    grad_projected = jnp.concatenate([grad_conv_rows, grad_gate_rows[None]], axis=0).astype(
        jnp.bfloat16
    )
    grad_mix = jnp.einsum(
        "td,jtc->jdc", normed1_low, grad_projected, preferred_element_type=jnp.float32
    )
    grad_normed1 = head_total(
        jnp.einsum("jtc,jdc->td", grad_projected, mix_again, preferred_element_type=jnp.float32)
    )
    grad_rows1, grad_norm1 = token_norm_back(token_rows, inverse1, norm1_gain, grad_normed1)
    grad_tokens = grad_hidden + grad_rows1
    mix_part, up_part, out_part, down_part = (
        lax.psum_scatter(grad_mix, "seq", scatter_dimension=1, tiled=True),
        lax.psum_scatter(grad_up, "seq", scatter_dimension=1, tiled=True),
        lax.psum_scatter(grad_out, "seq", scatter_dimension=1, tiled=True),
        lax.psum_scatter(grad_down, "seq", scatter_dimension=1, tiled=True),
    )
    conv_total, gap_total, group_total, norm1_total, norm2_total = lax.psum(
        (grad_conv, grad_gap, grad_group, grad_norm1, grad_norm2), "seq"
    )
    inverse_rms = jnp.stack([inverse1[:, 0], inverse2[:, 0]])
    return (
        block_out,
        grad_tokens,
        norm1_total,
        mix_part,
        conv_total,
        gap_total,
        group_total,
        out_part,
        norm2_total,
        up_part,
        down_part,
        inverse_rms,
    )


def solution(mesh):
    in_specs = (
        P("seq", None),
        P(),
        P(None, "seq", "head"),
        P(None, None, "head"),
        P("head"),
        P("head"),
        P("head", "seq"),
        P(),
        P(None, "seq", "head"),
        P("head", "seq"),
        P("seq", None),
    )
    out_specs = (
        P("seq", None),
        P("seq", None),
        P(),
        P(None, "seq", "head"),
        P(None, None, "head"),
        P("head"),
        P("head"),
        P("head", "seq"),
        P(),
        P(None, "seq", "head"),
        P("head", "seq"),
        P(None, "seq"),
    )
    return jax.shard_map(shards, mesh=mesh, in_specs=in_specs, out_specs=out_specs, check_vma=False)
```

profile of v0, /device:TPU:10, one launch (start us, length us, event | category | flops | bytes accessed | tf_op | source)
XLA Modules:
  0.0 3646.1 jit_solution(11405974941305117379)
XLA Ops:
  9.8 191.8 %all-gather.13.cloned.1.call-done = bf16[4,2048,1024]{2,1,0:T(8,128)(2,1)} async-done(((bf16[4,128,1024]{2,1,0:T(8,128)(2,1)}), bf16[4,2048,1024]{2,1,0:T(8,128)(2,1)}) %all-gather.13.cloned.1.call-update) | async-done | bytes 16777232 | tf_op jit(solution)/shard_map/all_gather | solution.py:154
  218.7 12.9 fusion.119
  235.8 31.4 all_gather.47
  270.4 77.4 %all-gather.29.cloned.1.call-done = f32[128,128,128]{2,1,0:T(8,128)} async-done(((f32[8,128,128]{2,1,0:T(8,128)}), f32[128,128,128]{2,1,0:T(8,128)}) %all-gather.29.cloned.1.call-update) | async-done | bytes 8388624 | tf_op jit(solution)/shard_map/all_gather | solution.py:21
  347.8 22.9 while.70
  386.4 50.0 %all-gather.15.cloned.1.call-done = bf16[1024,2048]{1,0:T(8,128)(2,1)} async-done(((bf16[1024,128]{1,0:T(8,128)(2,1)}), bf16[1024,2048]{1,0:T(8,128)(2,1)}) %all-gather.15.cloned.1.call-update) | async-done | bytes 4194320 | tf_op jit(solution)/shard_map/all_gather | solution.py:156
  464.2 250.8 %all-gather.19.cloned.1.call-done = bf16[2,2048,2816]{2,1,0:T(8,128)(2,1)} async-done(((bf16[2,128,2816]{2,1,0:T(8,128)(2,1)}), bf16[2,2048,2816]{2,1,0:T(8,128)(2,1)}) %all-gather.19.cloned.1.call-update) | async-done | bytes 23068688 | tf_op jit(solution)/shard_map/all_gather | solution.py:155
  715.0 12.4 convolution_bitcast_fusion.6
  727.4 170.8 %all-gather.21.cloned.1.call-done = bf16[2816,2048]{1,0:T(8,128)(2,1)} async-done(((bf16[2816,128]{1,0:T(8,128)(2,1)}), bf16[2816,2048]{1,0:T(8,128)(2,1)}) %all-gather.21.cloned.1.call-update) | async-done | bytes 11534352 | tf_op jit(solution)/shard_map/all_gather | solution.py:157
  898.3 10.1 fusion.59
  909.5 12.9 convolution_bitcast_fusion.8
  932.4 12.5 reduce-scatter.11.cloned.1.call-done
  945.0 11.6 all-gather.25.cloned.1.call-done
  988.3 109.4 %all-gather.31.cloned.1.call-done = f32[128,128,128]{2,1,0:T(8,128)} async-done(((f32[8,128,128]{2,1,0:T(8,128)}), f32[128,128,128]{2,1,0:T(8,128)}) %all-gather.31.cloned.1.call-update) | async-done | bytes 8388624 | tf_op jit(solution)/shard_map/all_gather | solution.py:21
  1097.6 33.4 while.71
  1134.4 37.0 %while.68 = (s32[]{:T(128)}, f32[8,128,128]{2,1,0:T(8,128)S(1)}, f32[2,64,8,128]{3,2,1,0:T(8,128)}, f32[2,64,8,128]{3,2,1,0:T(8,128)}, f32[2,64,8,128]{3,2,1,0:T...) while((s32[]{:T(128)}, f32[8,128,128]{2,1,0:T(8,128)S(1)}, ...), condition=%wide.region_22.23_spmd, body=%wide.region_17.22_spmd.sunk | while | flops 665260032 | bytes 41624012 | solution.py:100
  1187.2 12.4 convolution_bitcast_fusion.7
  1222.9 13.4 convolution_bitcast_fusion.5
  1237.7 19.0 convolution_bitcast_fusion.4
  1275.8 58.3 %all-reduce.16.cloned.1.call-done = (f32[2048]{0:T(1024)}, f32[3,4,1024]{2,0,1:T(4,128)}, f32[1024]{0:T(1024)}, f32[1024]{0:T(1024)}, f32[2048]{0:T(1024)}) async-done(((f32[2048]{0:T(1024)}, f32[3,4,1024]{2,0,1:T(4,128)}, f32[1024]{0:T(1024)}, f32[1024]{0:T(1024)}, f32[2048]{0:T(1024)}), (f32[2048]{0:T(1024)}, f32[3,4,1024]{2,0,1:T(4,128)}, f32[1024]{0:T(1024)}, f32[1024]{0:T(1024)}, ...) | async-done | bytes 73744 | tf_op jit(solution)/shard_map/psum | solution.py:260
  1335.6 690.0 %reduce-scatter.17.cloned.1.call-done = f32[4,128,1024]{1,2,0:T(8,128)} async-done(((f32[4,2048,1024]{1,2,0:T(8,128)}), f32[4,128,1024]{1,2,0:T(8,128)}) %reduce-scatter.17.cloned.1.call-update) | async-done | bytes 2097168 | tf_op jit(solution)/shard_map/reduce_scatter | solution.py:255
  2028.4 942.6 %reduce-scatter.21.cloned.1.call-done = f32[2,128,2816]{1,2,0:T(8,128)} async-done(((f32[2,2048,2816]{1,2,0:T(8,128)}), f32[2,128,2816]{1,2,0:T(8,128)}) %reduce-scatter.21.cloned.1.call-update) | async-done | bytes 2883600 | tf_op jit(solution)/shard_map/reduce_scatter | solution.py:256
  2974.4 180.3 %reduce-scatter.19.cloned.1.call-done = f32[1024,128]{1,0:T(8,128)} async-done(((f32[1024,2048]{1,0:T(8,128)}), f32[1024,128]{1,0:T(8,128)}) %reduce-scatter.19.cloned.1.call-update) | async-done | bytes 524304 | tf_op jit(solution)/shard_map/reduce_scatter | solution.py:257
  3154.7 482.1 %reduce-scatter.23.cloned.1.call-done = f32[2816,128]{1,0:T(8,128)} async-done(((f32[2816,2048]{1,0:T(8,128)}), f32[2816,128]{1,0:T(8,128)}) %reduce-scatter.23.cloned.1.call-update) | async-done | bytes 1441808 | tf_op jit(solution)/shard_map/reduce_scatter | solution.py:258
  (449 shorter events, 285.5 us)
Async XLA Ops:
  7.2 194.4 %all-gather.13.cloned.1.call-start = ((), (), s32[]{:S(2)}) async-start(), calls=%async_computation.8 | async-start | bytes 17825792 | tf_op jit(solution)/shard_map/all_gather | solution.py:154
  7.9 339.9 %all-gather.29.cloned.1.call-start = ((), (), s32[]{:S(2)}) async-start(), calls=%async_computation.24 | async-start | bytes 8912896 | tf_op jit(solution)/shard_map/all_gather | solution.py:21
  209.8 5.7 collective-permute-start
  235.0 201.5 %all-gather.15.cloned.1.call-start = ((), (), s32[]{:S(2)}) async-start(), calls=%async_computation.9 | async-start | bytes 4456448 | tf_op jit(solution)/shard_map/all_gather | solution.py:156
  235.7 214.6 %reduce-scatter.9.cloned.1.call-start = ((), (), s32[]{:S(2)}) async-start(), calls=%async_computation.10 | async-start | bytes 1572864 | tf_op jit(solution)/shard_map/reduce_scatter | solution.py:136
  440.4 21.7 all-gather.17.cloned.1.call-start
  450.3 264.7 %all-gather.19.cloned.1.call-start = ((), (), s32[]{:S(2)}) async-start(), calls=%async_computation.12 | async-start | bytes 24510464 | tf_op jit(solution)/shard_map/all_gather | solution.py:155
  450.9 447.4 %all-gather.21.cloned.1.call-start = ((), (), s32[]{:S(2)}) async-start(), calls=%async_computation.13 | async-start | bytes 12255232 | tf_op jit(solution)/shard_map/all_gather | solution.py:157
  451.7 480.7 %reduce-scatter.13.cloned.1.call-start = ((), (), s32[]{:S(2)}) async-start(), calls=%async_computation.16 | async-start | bytes 1572864 | tf_op jit(solution)/shard_map/reduce_scatter | solution.py:136
  922.4 22.5 reduce-scatter.11.cloned.1.call-start
  929.6 27.0 all-gather.25.cloned.1.call-start
  932.4 36.1 all-gather.23.cloned.1.call-start
  944.9 152.7 %all-gather.31.cloned.1.call-start = ((), (), s32[]{:S(2)}) async-start(), calls=%async_computation.25 | async-start | bytes 8912896 | tf_op jit(solution)/shard_map/all_gather | solution.py:21
  985.1 223.9 %reduce-scatter.15.cloned.1.call-start = ((), (), s32[]{:S(2)}) async-start(), calls=%async_computation.18 | async-start | bytes 1572864 | tf_op jit(solution)/shard_map/reduce_scatter | solution.py:136
  1180.2 6.8 collective-permute-start.1
  1199.6 21.0 all-gather.27.cloned.1.call-start
  1209.1 125.0 %all-reduce.16.cloned.1.call-start = ((), (), s32[]{:S(2)}) async-start(), calls=%async_computation.26 | async-start | bytes 180224 | tf_op jit(solution)/shard_map/psum | solution.py:260
  1222.8 802.7 %reduce-scatter.17.cloned.1.call-start = ((), (), s32[]{:S(2)}) async-start(), calls=%async_computation.20 | async-start | bytes 35651584 | tf_op jit(solution)/shard_map/reduce_scatter | solution.py:255
  1236.3 1734.7 %reduce-scatter.21.cloned.1.call-start = ((), (), s32[]{:S(2)}) async-start(), calls=%async_computation.22 | async-start | bytes 49020928 | tf_op jit(solution)/shard_map/reduce_scatter | solution.py:256
  1256.7 1898.0 %reduce-scatter.19.cloned.1.call-start = ((), (), s32[]{:S(2)}) async-start(), calls=%async_computation.21 | async-start | bytes 8912896 | tf_op jit(solution)/shard_map/reduce_scatter | solution.py:257
  1262.5 2374.2 %reduce-scatter.23.cloned.1.call-start = ((), (), s32[]{:S(2)}) async-start(), calls=%async_computation.23 | async-start | bytes 24510464 | tf_op jit(solution)/shard_map/reduce_scatter | solution.py:258
  2028.4 1608.9 %copy-start.73 = (f32[1024]{0:T(1024)S(1)}, f32[1024]{0:T(1024)}, u32[]{:S(2)}) copy-start(f32[1024]{0:T(1024)} %get-tuple-element.1199) | copy-start | bytes 12292
  2028.4 1609.5 %copy-start.72 = (f32[1024]{0:T(1024)S(1)}, f32[1024]{0:T(1024)}, u32[]{:S(2)}) copy-start(f32[1024]{0:T(1024)} %get-tuple-element.1200) | copy-start | bytes 12292
  2028.4 1610.1 %copy-start.66 = (f32[2048]{0:T(1024)S(1)}, f32[2048]{0:T(1024)}, u32[]{:S(2)}) copy-start(f32[2048]{0:T(1024)} %get-tuple-element.1202) | copy-start | bytes 24580
  (87 other events, 3335.2 us)
Sparse Core Ops, SparseCore 0:
  10.8 190.7 all-gather.12
  235.1 112.6 all-gather.28
  350.5 85.8 all-gather.14
  440.5 9.7 reduce-scatter.8
  451.8 10.2 all-gather.16
  465.0 249.9 all-gather.18
  718.1 180.1 all-gather.20
  922.5 9.8 reduce-scatter.12
  935.2 9.6 reduce-scatter.10
  946.4 10.1 all-gather.24
  958.2 10.1 all-gather.22
  985.2 112.3 all-gather.30
  1199.7 9.2 reduce-scatter.14
  1210.4 10.1 all-gather.26
  1227.8 106.2 all-reduce.15
  1336.3 689.1 reduce-scatter.16
  2027.7 943.2 reduce-scatter.20
  2973.7 180.8 reduce-scatter.18
  3157.6 479.1 reduce-scatter.22
where the time goes:
time: 3660 us; the launch traced here: 3650 us
  waiting for transfers between devices  3290 us (90%)
  matrix products  140 us (4%)
  other arithmetic  105 us (3%)
  local copies, waits for them, and re-layouts  56.5 us (2%)
    reduce_scatter x1, waiting for transfers between devices, shards(): lax.psum_scatter(grad_up, 'seq', scatter_dimension=1, tiled=True)  943 us
    reduce_scatter x1, waiting for transfers between devices, shards(): lax.psum_scatter(grad_mix, 'seq', scatter_dimension=1, tiled=True)  690 us
    reduce_scatter x1, waiting for transfers between devices, shards(): lax.psum_scatter(grad_down, 'seq', scatter_dimension=1, tiled=True)  482 us
    all_gather x1, waiting for transfers between devices, shards(): lax.all_gather(up_pair, 'seq', axis=1, tiled=True)  251 us
    all_gather x1, waiting for transfers between devices, shards(): lax.all_gather(mix_weight, 'seq', axis=1, tiled=True)  192 us
    all_gather x2, waiting for transfers between devices, carried_in(): everything = jax.tree.map(lambda part: lax.all_gather(part, axis), array)  187 us
    reduce_scatter x1, waiting for transfers between devices, shards(): lax.psum_scatter(grad_out, 'seq', scatter_dimension=1, tiled=True)  180 us
    all_gather x1, waiting for transfers between devices, shards(): lax.all_gather(down_weight, 'seq', axis=1, tiled=True)  171 us
  transfers between devices with their start and end apart: 21, of which 21 were waited for; matrix products, arithmetic and copies ran while one was open for 3% of the time, Pallas kernels for 0%

commit v1 on v0

--- a/solution.py
+++ b/solution.py
@@ -8,6 +8,28 @@
 EPS_TOKEN = 1e-06
 EPS_GROUP = 1e-05
 HIGH = lax.Precision.HIGHEST
+
+
+def laid_out(pieces, dim):
+    pieces = jnp.moveaxis(pieces, 0, dim)
+    dims = pieces.shape
+    return pieces.reshape(*dims[:dim], dims[dim] * dims[dim + 1], *dims[dim + 2 :])
+
+
+def ring_gather(x, axis, dim):
+    size = lax.axis_size(axis)
+    pairs = [(i, (i + 1) % size) for i in range(size)]
+    back = [(b, a) for a, b in pairs]
+    lower, upper = ([], [])
+    for turn in range(size - 1):
+        if turn % 2 == 0:
+            lower.append(lax.ppermute(lower[-1] if lower else x, axis, pairs))
+        else:
+            upper.append(lax.ppermute(upper[-1] if upper else x, axis, back))
+    blocks = jnp.stack([*lower[::-1], x, *upper])
+    shift = lax.axis_index(axis) - len(lower)
+    blocks = blocks[(jnp.arange(size) - shift) % size]
+    return laid_out(blocks, dim)
 
 
 def from_behind(value, axis, steps):
@@ -152,7 +174,7 @@
 ):
     mix_full, up_full, out_full, down_full = (
         lax.all_gather(mix_weight, "seq", axis=1, tiled=True),
-        lax.all_gather(up_pair, "seq", axis=1, tiled=True),
+        ring_gather(up_pair, "seq", 1),
         lax.all_gather(out_weight, "seq", axis=1, tiled=True),
         lax.all_gather(down_weight, "seq", axis=1, tiled=True),
     )

time: 3660 us -> 3920 us (1.071)
  waiting for transfers between devices: 3290 us -> 3440 us
  local copies, waits for them, and re-layouts: 56.5 us -> 132 us
  starting transfers between devices: 7.93 us -> 52 us
    ppermute x0 -> x15, waiting for transfers between devices: none -> 530 us  [the longest x8 406 us: ring_gather(): lower.append(lax.ppermute(lower[-1] if lower else x, axis, pairs))]
    all_gather x1, waiting for transfers between devices: 251 us -> 62 us  [shards(): lax.all_gather(up_pair, 'seq', axis=1, tiled=True)]
    all_gather x1, waiting for transfers between devices: 171 us -> 0.01 us  [shards(): lax.all_gather(down_weight, 'seq', axis=1, tiled=True)]
  transfers between devices with their start and end apart: 21 -> 36, of which waited for: 21 -> 32; matrix products, arithmetic and copies ran while one was open for 3% -> 5% of each run, Pallas kernels for 0% -> 0%
where the time goes in v1:
time: 3920 us; the launch traced here: 3910 us
  waiting for transfers between devices  3440 us (88%)
  matrix products  141 us (4%)
  local copies, waits for them, and re-layouts  132 us (3%)
  other arithmetic  98.5 us (3%)
  starting transfers between devices  52 us (1%)
    reduce_scatter x1, waiting for transfers between devices, shards(): lax.psum_scatter(grad_up, 'seq', scatter_dimension=1, tiled=True)  943 us
    reduce_scatter x1, waiting for transfers between devices, shards(): lax.psum_scatter(grad_mix, 'seq', scatter_dimension=1, tiled=True)  690 us
    reduce_scatter x1, waiting for transfers between devices, shards(): lax.psum_scatter(grad_down, 'seq', scatter_dimension=1, tiled=True)  482 us
    ppermute x8, waiting for transfers between devices, ring_gather(): lower.append(lax.ppermute(lower[-1] if lower else x, axis, pairs))  406 us
    all_gather x1, waiting for transfers between devices, shards(): lax.all_gather(mix_weight, 'seq', axis=1, tiled=True)  191 us
    all_gather x2, waiting for transfers between devices, carried_in(): everything = jax.tree.map(lambda part: lax.all_gather(part, axis), array)  188 us
    reduce_scatter x1, waiting for transfers between devices, shards(): lax.psum_scatter(grad_out, 'seq', scatter_dimension=1, tiled=True)  180 us
    ppermute x7, waiting for transfers between devices, ring_gather(): upper.append(lax.ppermute(upper[-1] if upper else x, axis, back))  124 us
  transfers between devices with their start and end apart: 36, of which 32 were waited for; matrix products, arithmetic and copies ran while one was open for 5% of the time, Pallas kernels for 0%

profile of v1, /device:TPU:10, one launch (start us, length us, event | category | flops | bytes accessed | tf_op | source)
XLA Modules:
  0.0 3909.5 jit_solution(3483347788495604902)
XLA Ops:
  10.8 190.7 %all-gather.13.cloned.1.call-done = bf16[4,2048,1024]{2,1,0:T(8,128)(2,1)} async-done(((bf16[4,128,1024]{2,1,0:T(8,128)(2,1)}), bf16[4,2048,1024]{2,1,0:T(8,128)(2,1)}) %all-gather.13.cloned.1.call-update) | async-done | bytes 16777232 | tf_op jit(solution)/shard_map/all_gather | solution.py:176
  224.0 31.4 all_gather.46
  257.5 78.5 %all-gather.29.cloned.1.call-done = f32[128,128,128]{2,1,0:T(8,128)} async-done(((f32[8,128,128]{2,1,0:T(8,128)}), f32[128,128,128]{2,1,0:T(8,128)}) %all-gather.29.cloned.1.call-update) | async-done | bytes 8388624 | tf_op jit(solution)/shard_map/all_gather | solution.py:43
  336.0 22.9 while.70
  379.6 45.1 %all-gather.15.cloned.1.call-done = bf16[1024,2048]{1,0:T(8,128)(2,1)} async-done(((bf16[1024,128]{1,0:T(8,128)(2,1)}), bf16[1024,2048]{1,0:T(8,128)(2,1)}) %all-gather.15.cloned.1.call-update) | async-done | bytes 4194320 | tf_op jit(solution)/shard_map/all_gather | solution.py:178
  441.4 40.3 %collective-permute-done.1 = bf16[2,128,2816]{2,1,0:T(8,128)(2,1)S(1)} collective-permute-done((bf16[2,128,2816]{2,1,0:T(8,128)(2,1)}, bf16[2,128,2816]{2,1,0:T(8,128)(2,1)S(1)}, u32[]{:S(2)}, u32[]{:S(2)}) %collective-permute-start.1) | collective-permute-done | bytes 1441824 | tf_op jit(solution)/shard_map/ppermute | solution.py:26
  485.5 59.0 %collective-permute-done.2 = bf16[2,128,2816]{2,1,0:T(8,128)(2,1)S(1)} collective-permute-done((bf16[2,128,2816]{2,1,0:T(8,128)(2,1)S(1)}, bf16[2,128,2816]{2,1,0:T(8,128)(2,1)S(1)}, u32[]{:S(2)}, u32[]{:S(2)}) %collective-permute-start.2) | collective-permute-done | bytes 1441824 | tf_op jit(solution)/shard_map/ppermute | solution.py:26
  551.8 69.1 %collective-permute-done.3 = bf16[2,128,2816]{2,1,0:T(8,128)(2,1)S(1)} collective-permute-done((bf16[2,128,2816]{2,1,0:T(8,128)(2,1)S(1)}, bf16[2,128,2816]{2,1,0:T(8,128)(2,1)S(1)}, u32[]{:S(2)}, u32[]{:S(2)}) %collective-permute-start.3) | collective-permute-done | bytes 1441824 | tf_op jit(solution)/shard_map/ppermute | solution.py:26
  623.6 91.6 %collective-permute-done.4 = bf16[2,128,2816]{2,1,0:T(8,128)(2,1)S(1)} collective-permute-done((bf16[2,128,2816]{2,1,0:T(8,128)(2,1)S(1)}, bf16[2,128,2816]{2,1,0:T(8,128)(2,1)S(1)}, u32[]{:S(2)}, u32[]{:S(2)}) %collective-permute-start.4) | collective-permute-done | bytes 1441824 | tf_op jit(solution)/shard_map/ppermute | solution.py:26
  736.3 57.6 %collective-permute-done.5 = bf16[2,128,2816]{2,1,0:T(8,128)(2,1)S(1)} collective-permute-done((bf16[2,128,2816]{2,1,0:T(8,128)(2,1)S(1)}, bf16[2,128,2816]{2,1,0:T(8,128)(2,1)S(1)}, u32[]{:S(2)}, u32[]{:S(2)}) %collective-permute-start.5) | collective-permute-done | bytes 1441824 | tf_op jit(solution)/shard_map/ppermute | solution.py:26
  799.2 27.3 collective-permute-done.6
  838.4 37.6 collective-permute-done.13
  878.4 30.7 collective-permute-done.7
  916.5 59.5 %collective-permute-done.14 = bf16[2,128,2816]{2,1,0:T(8,128)(2,1)} collective-permute-done((bf16[2,128,2816]{2,1,0:T(8,128)(2,1)}, bf16[2,128,2816]{2,1,0:T(8,128)(2,1)}, u32[]{:S(2)}, u32[]{:S(2)}) %collective-permute-start.14) | collective-permute-done | bytes 1441824 | tf_op jit(solution)/shard_map/ppermute | solution.py:28
  976.0 30.1 collective-permute-done.8
  1102.5 62.0 %all-gather.23.cloned.1.call-done = bf16[2,2048,2816]{2,1,0:T(8,128)(2,1)} async-done(((bf16[2,128,2816]{2,1,0:T(8,128)(2,1)}), bf16[2,2048,2816]{2,1,0:T(8,128)(2,1)}) %all-gather.23.cloned.1.call-update) | async-done | bytes 23068688 | tf_op jit(solution)/shard_map/all_gather | solution.py:225
  1249.1 109.5 %all-gather.31.cloned.1.call-done = f32[128,128,128]{2,1,0:T(8,128)} async-done(((f32[8,128,128]{2,1,0:T(8,128)}), f32[128,128,128]{2,1,0:T(8,128)}) %all-gather.31.cloned.1.call-update) | async-done | bytes 8388624 | tf_op jit(solution)/shard_map/all_gather | solution.py:43
  1358.7 33.4 while.71
  1395.4 39.4 %while.68 = (s32[]{:T(128)}, f32[8,128,128]{2,1,0:T(8,128)S(1)}, f32[2,64,8,128]{3,2,1,0:T(8,128)}, f32[2,64,8,128]{3,2,1,0:T(8,128)}, f32[2,64,8,128]{3,2,1,0:T...) while((s32[]{:T(128)}, f32[8,128,128]{2,1,0:T(8,128)S(1)}, ...), condition=%wide.region_22.23_spmd, body=%wide.region_17.22_spmd.sunk | while | flops 665260032 | bytes 37429652 | solution.py:122
  1539.2 58.3 %all-reduce.16.cloned.1.call-done = (f32[2048]{0:T(1024)}, f32[3,4,1024]{2,0,1:T(4,128)}, f32[1024]{0:T(1024)}, f32[1024]{0:T(1024)}, f32[2048]{0:T(1024)}) async-done(((f32[2048]{0:T(1024)}, f32[3,4,1024]{2,0,1:T(4,128)}, f32[1024]{0:T(1024)}, f32[1024]{0:T(1024)}, f32[2048]{0:T(1024)}), (f32[2048]{0:T(1024)}, f32[3,4,1024]{2,0,1:T(4,128)}, f32[1024]{0:T(1024)}, f32[1024]{0:T(1024)}, ...) | async-done | bytes 73744 | tf_op jit(solution)/shard_map/psum | solution.py:282
  1599.0 690.0 %reduce-scatter.17.cloned.1.call-done = f32[4,128,1024]{1,2,0:T(8,128)} async-done(((f32[4,2048,1024]{1,2,0:T(8,128)}), f32[4,128,1024]{1,2,0:T(8,128)}) %reduce-scatter.17.cloned.1.call-update) | async-done | bytes 2097168 | tf_op jit(solution)/shard_map/reduce_scatter | solution.py:277
  2291.8 942.6 %reduce-scatter.21.cloned.1.call-done = f32[2,128,2816]{1,2,0:T(8,128)} async-done(((f32[2,2048,2816]{1,2,0:T(8,128)}), f32[2,128,2816]{1,2,0:T(8,128)}) %reduce-scatter.21.cloned.1.call-update) | async-done | bytes 2883600 | tf_op jit(solution)/shard_map/reduce_scatter | solution.py:278
  3237.8 180.3 %reduce-scatter.19.cloned.1.call-done = f32[1024,128]{1,0:T(8,128)} async-done(((f32[1024,2048]{1,0:T(8,128)}), f32[1024,128]{1,0:T(8,128)}) %reduce-scatter.19.cloned.1.call-update) | async-done | bytes 524304 | tf_op jit(solution)/shard_map/reduce_scatter | solution.py:279
  3418.0 482.1 %reduce-scatter.23.cloned.1.call-done = f32[2816,128]{1,0:T(8,128)} async-done(((f32[2816,2048]{1,0:T(8,128)}), f32[2816,128]{1,0:T(8,128)}) %reduce-scatter.23.cloned.1.call-update) | async-done | bytes 1441808 | tf_op jit(solution)/shard_map/reduce_scatter | solution.py:280
  (507 shorter events, 532.3 us)
Async XLA Ops:
  7.2 194.4 %all-gather.13.cloned.1.call-start = ((), (), s32[]{:S(2)}) async-start(), calls=%async_computation.8 | async-start | bytes 17825792 | tf_op jit(solution)/shard_map/all_gather | solution.py:176
  7.9 328.1 %all-gather.29.cloned.1.call-start = ((), (), s32[]{:S(2)}) async-start(), calls=%async_computation.24 | async-start | bytes 8912896 | tf_op jit(solution)/shard_map/all_gather | solution.py:43
  223.2 201.5 %all-gather.15.cloned.1.call-start = ((), (), s32[]{:S(2)}) async-start(), calls=%async_computation.9 | async-start | bytes 4456448 | tf_op jit(solution)/shard_map/all_gather | solution.py:178
  223.9 214.6 %reduce-scatter.9.cloned.1.call-start = ((), (), s32[]{:S(2)}) async-start(), calls=%async_computation.10 | async-start | bytes 1572864 | tf_op jit(solution)/shard_map/reduce_scatter | solution.py:158
  428.6 648.7 %all-gather.17.cloned.1.call-start = ((), (), s32[]{:S(2)}) async-start(), calls=%async_computation.11 | async-start | bytes 1572864 | tf_op jit(solution)/shard_map/all_gather | solution.py:159
  438.6 653.8 %all-gather.19.cloned.1.call-start = ((), (), s32[]{:S(2)}) async-start(), calls=%async_computation.12 | async-start | bytes 12255232 | tf_op jit(solution)/shard_map/all_gather | solution.py:179
  439.1 725.4 %all-gather.23.cloned.1.call-start = ((), (), s32[]{:S(2)}) async-start(), calls=%async_computation.15 | async-start | bytes 24510464 | tf_op jit(solution)/shard_map/all_gather | solution.py:225
  439.9 757.3 %reduce-scatter.13.cloned.1.call-start = ((), (), s32[]{:S(2)}) async-start(), calls=%async_computation.16 | async-start | bytes 1572864 | tf_op jit(solution)/shard_map/reduce_scatter | solution.py:158
  544.5 76.4 %collective-permute-start.3 = (bf16[2,128,2816]{2,1,0:T(8,128)(2,1)S(1)}, bf16[2,128,2816]{2,1,0:T(8,128)(2,1)S(1)}, u32[]{:S(2)}, u32[]{:S(2)}) collective-permute-start(bf16[2,128,2816]{2,1,0:T(8,128)(2,1)S(1)} %collective-permute-done.2), channel_id=1, source_target_pairs={{0,2},{2,4},{4,6},{6,8},{8,10},{10,12},{12,14},{14,16},{16,18},{18... | collective-permute-start | bytes 4325384 | tf_op jit(solution)/shard_map/ppermute | solution.py:26
  550.3 71.1 %collective-permute-start.10 = (bf16[2,128,2816]{2,1,0:T(8,128)(2,1)S(1)}, bf16[2,128,2816]{2,1,0:T(8,128)(2,1)S(1)}, u32[]{:S(2)}, u32[]{:S(2)}) collective-permute-start(bf16[2,128,2816]{2,1,0:T(8,128)(2,1)S(1)} %collective-permute-done.9), channel_id=1, source_target_pairs={{2,0},{4,2},{6,4},{8,6},{10,8},{12,10},{14,12},{16,14},{18,16},{20... | collective-permute-start | bytes 4325384 | tf_op jit(solution)/shard_map/ppermute | solution.py:28
  620.9 94.4 %collective-permute-start.4 = (bf16[2,128,2816]{2,1,0:T(8,128)(2,1)S(1)}, bf16[2,128,2816]{2,1,0:T(8,128)(2,1)S(1)}, u32[]{:S(2)}, u32[]{:S(2)}) collective-permute-start(bf16[2,128,2816]{2,1,0:T(8,128)(2,1)S(1)} %collective-permute-done.3), channel_id=1, source_target_pairs={{0,2},{2,4},{4,6},{6,8},{8,10},{10,12},{12,14},{14,16},{16,18},{18... | collective-permute-start | bytes 4325384 | tf_op jit(solution)/shard_map/ppermute | solution.py:26
  621.4 113.3 %collective-permute-start.11 = (bf16[2,128,2816]{2,1,0:T(8,128)(2,1)S(1)}, bf16[2,128,2816]{2,1,0:T(8,128)(2,1)S(1)}, u32[]{:S(2)}, u32[]{:S(2)}) collective-permute-start(bf16[2,128,2816]{2,1,0:T(8,128)(2,1)S(1)} %collective-permute-done.10), channel_id=1, source_target_pairs={{2,0},{4,2},{6,4},{8,6},{10,8},{12,10},{14,12},{16,14},{18,16},{20... | collective-permute-start | bytes 4325384 | tf_op jit(solution)/shard_map/ppermute | solution.py:28
  715.2 78.7 %collective-permute-start.5 = (bf16[2,128,2816]{2,1,0:T(8,128)(2,1)S(1)}, bf16[2,128,2816]{2,1,0:T(8,128)(2,1)S(1)}, u32[]{:S(2)}, u32[]{:S(2)}) collective-permute-start(bf16[2,128,2816]{2,1,0:T(8,128)(2,1)S(1)} %collective-permute-done.4), channel_id=1, source_target_pairs={{0,2},{2,4},{4,6},{6,8},{8,10},{10,12},{12,14},{14,16},{16,18},{18... | collective-permute-start | bytes 4325384 | tf_op jit(solution)/shard_map/ppermute | solution.py:26
  797.6 78.4 %collective-permute-start.13 = (bf16[2,128,2816]{2,1,0:T(8,128)(2,1)S(1)}, bf16[2,128,2816]{2,1,0:T(8,128)(2,1)}, u32[]{:S(2)}, u32[]{:S(2)}) collective-permute-start(bf16[2,128,2816]{2,1,0:T(8,128)(2,1)S(1)} %collective-permute-done.12), channel_id=1, source_target_pairs={{2,0},{4,2},{6,4},{8,6},{10,8},{12,10},{14,12},{16,14},{18,16},{20... | collective-permute-start | bytes 4325384 | tf_op jit(solution)/shard_map/ppermute | solution.py:28
  826.5 82.6 %collective-permute-start.7 = (bf16[2,128,2816]{2,1,0:T(8,128)(2,1)S(1)}, bf16[2,128,2816]{2,1,0:T(8,128)(2,1)}, u32[]{:S(2)}, u32[]{:S(2)}) collective-permute-start(bf16[2,128,2816]{2,1,0:T(8,128)(2,1)S(1)} %collective-permute-done.6), channel_id=1, source_target_pairs={{0,2},{2,4},{4,6},{6,8},{8,10},{10,12},{12,14},{14,16},{16,18},{18... | collective-permute-start | bytes 4325384 | tf_op jit(solution)/shard_map/ppermute | solution.py:26
  876.0 100.0 %collective-permute-start.14 = (bf16[2,128,2816]{2,1,0:T(8,128)(2,1)}, bf16[2,128,2816]{2,1,0:T(8,128)(2,1)}, u32[]{:S(2)}, u32[]{:S(2)}) collective-permute-start(bf16[2,128,2816]{2,1,0:T(8,128)(2,1)} %collective-permute-done.13), channel_id=1, source_target_pairs={{2,0},{4,2},{6,4},{8,6},{10,8},{12,10},{14,12},{16,14},{18,16},{20... | collective-permute-start | bytes 4325384 | tf_op jit(solution)/shard_map/ppermute | solution.py:28
  909.1 97.0 %collective-permute-start.8 = (bf16[2,128,2816]{2,1,0:T(8,128)(2,1)}, bf16[2,128,2816]{2,1,0:T(8,128)(2,1)}, u32[]{:S(2)}, u32[]{:S(2)}) collective-permute-start(bf16[2,128,2816]{2,1,0:T(8,128)(2,1)} %collective-permute-done.7), channel_id=1, source_target_pairs={{0,2},{2,4},{4,6},{6,8},{8,10},{10,12},{12,14},{14,16},{16,18},{18... | collective-permute-start | bytes 4325384 | tf_op jit(solution)/shard_map/ppermute | solution.py:26
  1206.5 152.1 %all-gather.31.cloned.1.call-start = ((), (), s32[]{:S(2)}) async-start(), calls=%async_computation.25 | async-start | bytes 8912896 | tf_op jit(solution)/shard_map/all_gather | solution.py:43
  1246.1 226.2 %reduce-scatter.15.cloned.1.call-start = ((), (), s32[]{:S(2)}) async-start(), calls=%async_computation.18 | async-start | bytes 1572864 | tf_op jit(solution)/shard_map/reduce_scatter | solution.py:158
  1472.4 125.1 %all-reduce.16.cloned.1.call-start = ((), (), s32[]{:S(2)}) async-start(), calls=%async_computation.26 | async-start | bytes 180224 | tf_op jit(solution)/shard_map/psum | solution.py:282
  1486.1 802.8 %reduce-scatter.17.cloned.1.call-start = ((), (), s32[]{:S(2)}) async-start(), calls=%async_computation.20 | async-start | bytes 35651584 | tf_op jit(solution)/shard_map/reduce_scatter | solution.py:277
  1499.6 1734.8 %reduce-scatter.21.cloned.1.call-start = ((), (), s32[]{:S(2)}) async-start(), calls=%async_computation.22 | async-start | bytes 49020928 | tf_op jit(solution)/shard_map/reduce_scatter | solution.py:278
  1520.1 1897.9 %reduce-scatter.19.cloned.1.call-start = ((), (), s32[]{:S(2)}) async-start(), calls=%async_computation.21 | async-start | bytes 8912896 | tf_op jit(solution)/shard_map/reduce_scatter | solution.py:279
  1526.0 2374.2 %reduce-scatter.23.cloned.1.call-start = ((), (), s32[]{:S(2)}) async-start(), calls=%async_computation.23 | async-start | bytes 24510464 | tf_op jit(solution)/shard_map/reduce_scatter | solution.py:280
  (106 other events, 8515.1 us)
Sparse Core Ops, SparseCore 0:
  10.8 190.7 all-gather.12
  223.3 112.6 all-gather.28
  338.7 85.8 all-gather.14
  428.7 9.8 reduce-scatter.8
  440.0 10.1 all-gather.16
  453.2 336.8 all-gather.18
  793.2 371.2 all-gather.22
  1177.9 9.1 reduce-scatter.12
  1197.3 9.1 reduce-scatter.10
  1208.0 10.1 all-gather.24
  1219.8 10.1 all-gather.20
  1246.3 112.3 all-gather.30
  1463.1 9.2 reduce-scatter.14
  1473.7 10.1 all-gather.26
  1491.1 106.2 all-reduce.15
  1599.7 689.1 reduce-scatter.16
  2291.1 943.2 reduce-scatter.20
  3237.1 180.8 reduce-scatter.18
  3420.9 479.1 reduce-scatter.22
